TPU v7x, 256 devices: a whole 4x4x8 slice. The times are simulated.
256 devices in a mesh: cam: 8 (over z_lo, core), tile: 32 (over x, z_hi, y).
Axes of the slice: x: 4, y: 4, z: 8 (z_hi: 2, z_lo: 4; z = z_hi * 4 + z_lo), core: 2. Of those that a mesh axis runs over, the one named last changes fastest.
Arguments:
- queries: bfloat16 [8192, 256], P('tile'), as said below
- keys: bfloat16 [16384, 256], P(('cam', 'tile')), as said below
- values: bfloat16 [16384, 256], P(('cam', 'tile')), may hold values from -6 to 6
- grad_out: bfloat16 [8192, 256], P('tile'), may hold values from -6 to 6
- visible: int32 [64, 512], P('tile', 'cam'), may hold values from 0 to 1, as said below
- counts: int32 [512], P('cam'), may hold values from 2 to 32
Outputs:
- grad_queries: bfloat16 [8192, 256], P('tile')
- grad_keys: bfloat16 [16384, 256], P(('cam', 'tile'))
- grad_values: bfloat16 [16384, 256], P(('cam', 'tile'))
Inputs may be any that keep to these rules, and one draw needn't show every extreme that they name: Every tile has at least one visible block. `queries`: projected query features. `keys`: projected key features.
All inputs are finite; a program needn't handle non-finite values.
Results may differ from a plain program's by a relative error of at most 0.0052.
Values may be sent and summed in bfloat16 or wider, within the bound.
A program may use at most 128 MiB of HBM per device.

v0:
```python
import math
import jax
import jax.numpy as jnp
from jax import lax
from jax.sharding import PartitionSpec as P

H = 8


def shards(queries, keys, values, grad_out, visible, counts):
    row_count, width = queries.shape
    head_dim = width // H
    scale = 1.0 / math.sqrt(head_dim)
    key_all, value_all = (
        lax.all_gather(keys, "tile", axis=0, tiled=True),
        lax.all_gather(values, "tile", axis=0, tiled=True),
    )
    group = key_all.shape[0]
    block_count = counts.shape[0]
    block_keys = group // block_count
    slot_index = jnp.arange(group, dtype=jnp.int32) % block_keys
    key_valid = slot_index < jnp.repeat(counts, block_keys)
    tile_count = visible.shape[0]
    tile_rows = row_count // tile_count
    mask_tiles = (jnp.repeat(visible, block_keys, axis=1) == 1) & key_valid[None, :]
    per_step = 2
    step_count = tile_count // per_step
    step_rows = per_step * tile_rows
    query_blocks = queries.reshape(step_count, step_rows, H, head_dim)
    grad_blocks = grad_out.reshape(step_count, step_rows, H, head_dim)
    mask_blocks = mask_tiles.reshape(step_count, per_step, group)
    key_heads = key_all.reshape(group, H, head_dim)
    value_heads = value_all.reshape(group, H, head_dim)

    def scores_of(query_blk, key_mat):
        return (
            jnp.einsum("qhd,khd->hqk", query_blk, key_mat, preferred_element_type=jnp.float32)
            * scale
        )

    def row_mask(mask_blk):
        return jnp.repeat(mask_blk, tile_rows, axis=0)[None, :, :]

    def local_stats(inputs):
        query_blk, mask_blk = inputs
        scores = scores_of(query_blk, key_heads)
        allowed = row_mask(mask_blk)
        top = jnp.max(jnp.where(allowed, scores, -1e30), axis=-1)
        total = jnp.sum(jnp.where(allowed, jnp.exp(scores - top[..., None]), 0.0), axis=-1)
        return (top, total)

    local_top, local_total = lax.map(local_stats, (query_blocks, mask_blocks))
    global_top = lax.pmax(local_top, "cam")
    global_total = lax.psum(local_total * jnp.exp(local_top - global_top), "cam")
    lse_all = global_top + jnp.log(global_total)

    def probs_terms(query_blk, grad_blk, mask_blk, lse_blk, key_mat, value_mat):
        scores = scores_of(query_blk, key_mat)
        allowed = row_mask(mask_blk)
        probs = jnp.where(allowed, jnp.exp(scores - lse_blk[..., None]), 0.0)
        dprobs = jnp.einsum("qhd,khd->hqk", grad_blk, value_mat, preferred_element_type=jnp.float32)
        return (probs, dprobs)

    def local_delta(inputs):
        query_blk, grad_blk, mask_blk, lse_blk = inputs
        probs, dprobs = probs_terms(query_blk, grad_blk, mask_blk, lse_blk, key_heads, value_heads)
        return jnp.sum(probs * dprobs, axis=-1)

    delta_part = lax.map(local_delta, (query_blocks, grad_blocks, mask_blocks, lse_all))
    delta_all = lax.psum(delta_part, "cam")

    def rounded_terms(query_blk, grad_blk, mask_blk, lse_blk, delta_blk, key_mat, value_mat):
        probs, dprobs = probs_terms(query_blk, grad_blk, mask_blk, lse_blk, key_mat, value_mat)
        dscores = probs * (dprobs - delta_blk[..., None])
        return (probs.astype(jnp.bfloat16), dscores.astype(jnp.bfloat16))

    def query_grad_of(dscores_b):
        grad_q = (
            jnp.einsum("hqk,khd->qhd", dscores_b, key_heads, preferred_element_type=jnp.float32)
            * scale
        )
        return grad_q.reshape(step_rows, width)

    def grad_step(carry, inputs):
        query_blk, grad_blk, mask_blk, lse_blk, delta_blk = inputs
        probs_b, dscores_b = rounded_terms(
            query_blk, grad_blk, mask_blk, lse_blk, delta_blk, key_heads, value_heads
        )
        grad_k = (
            carry[0]
            + jnp.einsum("hqk,qhd->khd", dscores_b, query_blk, preferred_element_type=jnp.float32)
            * scale
        )
        grad_v = carry[1] + jnp.einsum(
            "hqk,qhd->khd", probs_b, grad_blk, preferred_element_type=jnp.float32
        )
        return ((grad_k, grad_v), query_grad_of(dscores_b))

    zero_kv = jnp.zeros((group, H, head_dim), jnp.float32)
    (grad_k, grad_v), query_parts = lax.scan(
        grad_step, (zero_kv, zero_kv), (query_blocks, grad_blocks, mask_blocks, lse_all, delta_all)
    )
    joined = jnp.concatenate((grad_k.reshape(group, width), grad_v.reshape(group, width)), axis=1)
    owned = lax.psum_scatter(joined, "tile", scatter_dimension=0, tiled=True)
    grad_queries = lax.psum(query_parts.reshape(row_count, width), "cam").astype(jnp.bfloat16)
    grad_keys = owned[:, :width].astype(jnp.bfloat16)
    grad_values = owned[:, width:].astype(jnp.bfloat16)
    return (grad_queries, grad_keys, grad_values)


def solution(mesh):
    in_specs = (
        P("tile", None),
        P(("cam", "tile"), None),
        P(("cam", "tile"), None),
        P("tile", None),
        P("tile", "cam"),
        P("cam"),
    )
    out_specs = (P("tile", None), P(("cam", "tile"), None), P(("cam", "tile"), None))
    return jax.shard_map(shards, mesh=mesh, in_specs=in_specs, out_specs=out_specs, check_vma=False)
```

profile of v0, /device:TPU:32, one launch (start us, length us, event | category | flops | bytes accessed | tf_op | source)
XLA Modules:
  0.0 469.4 jit_solution(15476085039806583543)
XLA Ops:
  7.2 0.7 all-gather.3.cloned.1.call-update
  7.9 0.7 all-gather.5.cloned.1.call-update
  8.7 0.7 broadcast_in_dim.83
  9.5 0.7 broadcast_compare_fusion
  10.3 0.1 eq.14
  10.4 1.0 copy.18
  11.4 1.0 copy.20
  12.4 81.8 %all-gather.3.cloned.1.call-done = bf16[2048,256]{1,0:T(8,128)(2,1)} async-done(((bf16[64,256]{1,0:T(8,128)(2,1)}), bf16[2048,256]{1,0:T(8,128)(2,1)}) %all-gather.3.cloned.1.call-update) | async-done | bytes 1048592 | tf_op jit(solution)/shard_map/all_gather | solution.py:15
  94.2 1.5 copy.19
  95.7 0.2 broadcast_in_dim.84
  95.9 3.3 select_reduce_fusion.1
  99.2 5.7 %copy-done = f32[8,256,2048]{2,1,0:T(8,128)} copy-done((f32[8,256,2048]{2,1,0:T(8,128)}, f32[8,256,2048]{2,1,0:T(8,128)S(1)}, u32[]{:S(2)}) %copy-start) | copy-done | bytes 16777240
  104.9 4.6 select_reduce_fusion
  109.5 11.9 %pmax.7 = f32[1,8,256]{2,1,0:T(8,128)S(1)} all-reduce(f32[1,8,256]{2,1,0:T(8,128)S(1)} %bitcast.44), channel_id=1, replica_groups=mesh['cam'=8,'tile'=32] {'cam'}, use_global_device_ids=true, to_apply=%region_1.2 | all-reduce | flops 2048 | bytes 16384 | tf_op jit(solution)/shard_map/pmax | solution.py:53
  121.4 14.3 %psum.21 = f32[1,8,256]{2,1,0:T(8,128)S(1)} all-reduce(f32[1,8,256]{2,1,0:T(8,128)S(1)} %bitcast_multiply_fusion), channel_id=1, replica_groups=mesh['cam'=8,'tile'=32] {'cam'}, use_global_device_ids=true, to_apply=%region_3.4 | all-reduce | flops 2048 | bytes 16384 | tf_op jit(solution)/shard_map/psum | solution.py:54
  135.7 9.1 %fusion.1 = f32[8,2048,32]{1,2,0:T(8,128)} fusion(bf16[256,8,32]{0,2,1:T(8,128)(2,1)S(1)} %bitcast.42, f32[8,256,2048]{2,1,0:T(8,128)} %copy-done, f32[8,256]{1,0:T(8,128)S(1)} %add_bitcast_fusion, pred[256,2048]{1,0:T(8,128)(4,1)S(1)} %bitcast.31), kind=kOutput, calls=%fused_computation.6 | convolution fusion | flops 285212672 | bytes 19537920 | tf_op jit(solution)/shard_map/while/body/eval_jaxpr/hqk,qhd->khd/dot_general | solution.py:94
  144.9 28.7 %all-gather.5.cloned.1.call-done = bf16[2048,256]{1,0:T(8,128)(2,1)} async-done(((bf16[64,256]{1,0:T(8,128)(2,1)}), bf16[2048,256]{1,0:T(8,128)(2,1)}) %all-gather.5.cloned.1.call-update) | async-done | bytes 1048592 | tf_op jit(solution)/shard_map/all_gather | solution.py:16
  173.6 1.5 copy.21
  175.1 12.6 %multiply_reduce_fusion = (f32[8,256]{1,0:T(8,128)S(1)}, f32[8,256,2048]{2,1,0:T(8,128)}) fusion(f32[8,256,2048]{2,1,0:T(8,128)} %copy-done, f32[8,256]{1,0:T(8,128)S(1)} %add_bitcast_fusion, pred[256,2048]{1,0:T(8,128)(4,1)S(1)} %bitcast.32, bf16[256,8,32]{0,2,1:T(8,128)(2,1)S(1)} %bitcast.43, bf16[2048,8,32]{0,2,1:T(8,128)(2,1)S(1)} %bitcast.37), kind=kOutput, calls=%fused_computation.1 | convolution fusion | flops 289404928 | bytes 35274752 | tf_op jit(solution)/shard_map/while/body/eval_jaxpr/qhd,khd->hqk/dot_general | solution.py:61
  187.7 12.1 %psum.22 = f32[8,256]{1,0:T(8,128)S(1)} all-reduce(f32[8,256]{1,0:T(8,128)S(1)} %get-tuple-element.60), channel_id=1, replica_groups=mesh['cam'=8,'tile'=32] {'cam'}, use_global_device_ids=true, to_apply=%region_5.6 | all-reduce | flops 2048 | bytes 16384 | tf_op jit(solution)/shard_map/psum | solution.py:70
  199.8 12.2 %multiply_convert_fusion = bf16[8,256,2048]{2,1,0:T(8,128)(2,1)S(1)} fusion(f32[8,256,2048]{2,1,0:T(8,128)} %get-tuple-element.61, f32[8,256,2048]{2,1,0:T(8,128)} %copy-done, f32[8,256]{1,0:T(8,128)S(1)} %psum.22, f32[8,256]{1,0:T(8,128)S(1)} %add_bitcast_fusion, pred[256,2048]{1,0:T(8,128)(4,1)S(1)} %bitcast.33), kind=kLoop, calls=%fused_computation | loop fusion | flops 25165824 | bytes 42483712 | tf_op jit(solution)/shard_map/while/body/eval_jaxpr/convert_element_type | solution.py:75
  212.0 3.2 copy-done.1
  215.2 1.5 convolution_multiply_fusion
  216.7 1.9 copy.23
  218.6 1.9 copy.24
  220.5 4.2 pad_maximum_fusion
  224.8 6.0 %convolution_multiply_fusion.1 = f32[8,256,32]{1,2,0:T(8,128)S(1)} fusion(bf16[8,256,2048]{2,1,0:T(8,128)(2,1)} %copy-done.1, bf16[2048,8,32]{0,2,1:T(8,128)(2,1)S(1)} %bitcast.36), kind=kOutput, calls=%fused_computation.10 | convolution fusion | flops 268500992 | bytes 9699328 | tf_op jit(solution)/shard_map/while/body/eval_jaxpr/hqk,khd->qhd/dot_general | solution.py:79
  230.8 0.1 copy.22
  230.9 33.8 %all-reduce.1 = bf16[256,256]{1,0:T(8,128)(2,1)} all-reduce(f32[256,256]{1,0:T(8,128)S(1)} %copy.22), channel_id=1, replica_groups=mesh['cam'=8,'tile'=32] {'cam'}, use_global_device_ids=true, to_apply=%region_6.7 | all-reduce | flops 65536 | bytes 393216 | tf_op jit(solution)/shard_map/psum | solution.py:105
  264.7 196.6 %reduce-scatter.2.cloned.1.call-done = f32[64,512]{1,0:T(8,128)} async-done(((f32[2048,512]{1,0:T(8,128)}), f32[64,512]{1,0:T(8,128)}) %reduce-scatter.2.cloned.1.call-update) | async-done | bytes 131088 | tf_op jit(solution)/shard_map/reduce_scatter | solution.py:104
  461.3 0.9 convert.4
  462.2 0.6 fusion.10
  (12 shorter events, 0.3 us)
Async XLA Ops:
  7.2 87.1 %all-gather.3.cloned.1.call-start = ((), (), s32[]{:S(2)}) async-start(), calls=%async_computation.1 | async-start | bytes 1081344 | tf_op jit(solution)/shard_map/all_gather | solution.py:15
  7.9 165.7 %all-gather.5.cloned.1.call-start = ((), (), s32[]{:S(2)}) async-start(), calls=%async_computation.2 | async-start | bytes 1081344 | tf_op jit(solution)/shard_map/all_gather | solution.py:16
  8.6 452.6 %reduce-scatter.2.cloned.1.call-start = ((), (), s32[]{:S(2)}) async-start(), calls=%async_computation.3 | async-start | bytes 4325376 | tf_op jit(solution)/shard_map/reduce_scatter | solution.py:104
  99.2 5.7 %copy-start = (f32[8,256,2048]{2,1,0:T(8,128)}, f32[8,256,2048]{2,1,0:T(8,128)S(1)}, u32[]{:S(2)}) copy-start(f32[8,256,2048]{2,1,0:T(8,128)S(1)} %get-tuple-element.59) | copy-start | bytes 50331652
  212.0 3.2 copy-start.1
Sparse Core Ops, SparseCore 0:
  11.4 82.7 all-gather.2
  97.6 75.8 all-gather.4
  224.9 236.3 reduce-scatter.1
where the time goes:
time: 470 us; the launch traced here: 469 us
  waiting for transfers between devices  308 us (66%)
  blocking collectives  72 us (15%)
  matrix products  32.5 us (7%)
  other arithmetic  22.7 us (5%)
  local copies, waits for them, and re-layouts  19.6 us (4%)
  between operations  13.9 us (3%)
    reduce_scatter x1, waiting for transfers between devices, shards(): owned = lax.psum_scatter(joined, 'tile', scatter_dimension=0, tiled=True)  197 us
    all_gather x1, waiting for transfers between devices, shards(): lax.all_gather(keys, 'tile', axis=0, tiled=True)  81.8 us
    psum x1, blocking collectives, shards(): lax.psum(query_parts.reshape(row_count, width), 'cam').astype(jnp.bfloat16)  33.8 us
    all_gather x1, waiting for transfers between devices, shards(): lax.all_gather(values, 'tile', axis=0, tiled=True)  28.7 us
    psum x1, blocking collectives, shards(): lax.psum(local_total * jnp.exp(local_top - global_top), 'cam')  14.3 us
    dot_general x1, matrix products, probs_terms(): jnp.einsum('qhd,khd->hqk', grad_blk, value_mat, preferred_element_type=jn...  12.6 us
    convert_element_type x1, other arithmetic, rounded_terms(): return (probs.astype(jnp.bfloat16), dscores.astype(jnp.bfloat16))  12.2 us
    psum x1, blocking collectives, shards(): delta_all = lax.psum(delta_part, 'cam')  12.1 us
  transfers between devices with their start and end apart: 3, of which 3 were waited for; matrix products, arithmetic and copies ran while one was open for 6% of the time, Pallas kernels for 0%

commit v1 on v0

--- a/solution.py
+++ b/solution.py
@@ -13,7 +13,9 @@
     scale = 1.0 / math.sqrt(head_dim)
     key_all, value_all = (
         lax.all_gather(keys, "tile", axis=0, tiled=True),
-        lax.all_gather(values, "tile", axis=0, tiled=True),
+        jnp.concatenate(
+            lax.all_to_all(jnp.stack([values] * lax.axis_size("tile")), "tile", 0, 0), axis=0
+        ),
     )
     group = key_all.shape[0]
     block_count = counts.shape[0]

time: 470 us -> 453 us (0.964)
  waiting for transfers between devices: 308 us -> 265 us
  starting transfers between devices: 0.11 us -> 13.1 us
  local copies, waits for them, and re-layouts: 19.6 us -> 28.2 us
    all_gather x1 -> x0, waiting for transfers between devices: 28.7 us -> none  [shards(): lax.all_gather(values, 'tile', axis=0, tiled=True)]
    all_to_all x0 -> x1, starting transfers between devices: none -> 13 us  [shards(): lax.all_to_all(jnp.stack([values] * lax.axis_size('tile')), 'tile', 0, 0)]
    all_gather x1, waiting for transfers between devices: 81.8 us -> 72.6 us  [shards(): lax.all_gather(keys, 'tile', axis=0, tiled=True)]
    reduce_scatter x1, waiting for transfers between devices: 197 us -> 191 us  [shards(): owned = lax.psum_scatter(joined, 'tile', scatter_dimension=0, tiled=True)]
    another operation x0 -> x2, local copies, waits for them, and re-layouts: none -> 5.24 us  [the longest x1 3.38 us: shards(): value_heads = value_all.reshape(group, H, head_dim)]
  transfers between devices with their start and end apart: 3 -> 3, of which waited for: 3 -> 2; matrix products, arithmetic and copies ran while one was open for 6% -> 7% of each run, Pallas kernels for 0% -> 0%
where the time goes in v1:
time: 453 us; the launch traced here: 450 us
  waiting for transfers between devices  265 us (58%)
  blocking collectives  74 us (16%)
  matrix products  32.5 us (7%)
  local copies, waits for them, and re-layouts  28.2 us (6%)
  other arithmetic  23.2 us (5%)
  between operations  14.2 us (3%)
  starting transfers between devices  13.1 us (3%)
    reduce_scatter x1, waiting for transfers between devices, shards(): owned = lax.psum_scatter(joined, 'tile', scatter_dimension=0, tiled=True)  191 us
    all_gather x1, waiting for transfers between devices, shards(): lax.all_gather(keys, 'tile', axis=0, tiled=True)  72.6 us
    psum x1, blocking collectives, shards(): lax.psum(query_parts.reshape(row_count, width), 'cam').astype(jnp.bfloat16)  33.9 us
    psum x1, blocking collectives, shards(): delta_all = lax.psum(delta_part, 'cam')  14.1 us
    psum x1, blocking collectives, shards(): lax.psum(local_total * jnp.exp(local_top - global_top), 'cam')  14.1 us
    all_to_all x1, starting transfers between devices, shards(): lax.all_to_all(jnp.stack([values] * lax.axis_size('tile')), 'tile', 0, 0)  13 us
    dot_general x1, matrix products, probs_terms(): jnp.einsum('qhd,khd->hqk', grad_blk, value_mat, preferred_element_type=jn...  12.6 us
    convert_element_type x1, other arithmetic, rounded_terms(): return (probs.astype(jnp.bfloat16), dscores.astype(jnp.bfloat16))  12.2 us
  transfers between devices with their start and end apart: 3, of which 2 were waited for; matrix products, arithmetic and copies ran while one was open for 7% of the time, Pallas kernels for 0%

profile of v1, /device:TPU:32, one launch (start us, length us, event | category | flops | bytes accessed | tf_op | source)
XLA Modules:
  0.0 449.9 jit_solution(843375833608808761)
XLA Ops:
  7.2 0.7 all-gather.2.cloned.1.call-update
  7.9 1.9 stack.2
  9.8 13.0 %all-to-all-start = ((bf16[32,64,256]{2,1,0:T(8,128)(2,1)}), bf16[32,64,256]{2,1,0:T(8,128)(2,1)S(1)}, u32[]{:S(2)}, u32[]{:S(2)}) async-start(bf16[32,64,256]{2,1,0:T(8,128)(2,1)} %stack.2), calls=%async_computation | async-start | bytes 2097152 | tf_op jit(solution)/shard_map/all_to_all | solution.py:17
  22.9 0.7 broadcast_in_dim.83
  23.7 0.7 broadcast_compare_fusion
  24.6 1.0 copy.25
  25.6 1.0 copy.27
  26.6 72.6 %all-gather.2.cloned.1.call-done = bf16[2048,256]{1,0:T(8,128)(2,1)} async-done(((bf16[64,256]{1,0:T(8,128)(2,1)}), bf16[2048,256]{1,0:T(8,128)(2,1)}) %all-gather.2.cloned.1.call-update) | async-done | bytes 1048592 | tf_op jit(solution)/shard_map/all_gather | solution.py:15
  99.3 1.5 copy.26
  100.8 0.2 broadcast_in_dim.84
  101.0 3.3 select_reduce_fusion.1
  104.2 5.7 %copy-done = f32[8,256,2048]{2,1,0:T(8,128)} copy-done((f32[8,256,2048]{2,1,0:T(8,128)}, f32[8,256,2048]{2,1,0:T(8,128)S(1)}, u32[]{:S(2)}) %copy-start) | copy-done | bytes 16777240
  109.9 4.6 %select_reduce_fusion = f32[8,256]{1,0:T(8,128)S(1)} fusion(f32[8,256,2048]{2,1,0:T(8,128)S(1)} %get-tuple-element.59, f32[8,256]{1,0:T(8,128)S(1)} %get-tuple-element.58, pred[256,2048]{1,0:T(8,128)(4,1)S(1)} %bitcast.31), kind=kLoop, calls=%fused_computation.3 | loop fusion | flops 16775168 | bytes 17317888 | tf_op jit(solution)/shard_map/while/body/eval_jaxpr/reduce_sum | solution.py:51
  114.5 11.9 %pmax.7 = f32[1,8,256]{2,1,0:T(8,128)S(1)} all-reduce(f32[1,8,256]{2,1,0:T(8,128)S(1)} %bitcast.44), channel_id=1, replica_groups=mesh['cam'=8,'tile'=32] {'cam'}, use_global_device_ids=true, to_apply=%region_1.2 | all-reduce | flops 2048 | bytes 16384 | tf_op jit(solution)/shard_map/pmax | solution.py:55
  126.5 14.1 %psum.21 = f32[1,8,256]{2,1,0:T(8,128)S(1)} all-reduce(f32[1,8,256]{2,1,0:T(8,128)S(1)} %bitcast_multiply_fusion), channel_id=1, replica_groups=mesh['cam'=8,'tile'=32] {'cam'}, use_global_device_ids=true, to_apply=%region_3.4 | all-reduce | flops 2048 | bytes 16384 | tf_op jit(solution)/shard_map/psum | solution.py:56
  140.6 9.1 %fusion.1 = f32[8,2048,32]{1,2,0:T(8,128)} fusion(bf16[256,8,32]{0,2,1:T(8,128)(2,1)S(1)} %bitcast.42, f32[8,256,2048]{2,1,0:T(8,128)} %copy-done, f32[8,256]{1,0:T(8,128)S(1)} %add_bitcast_fusion, pred[256,2048]{1,0:T(8,128)(4,1)S(1)} %bitcast.32), kind=kOutput, calls=%fused_computation.6 | convolution fusion | flops 285212672 | bytes 19537920 | tf_op jit(solution)/shard_map/while/body/eval_jaxpr/hqk,qhd->khd/dot_general | solution.py:96
  149.7 2.9 copy.31
  152.7 3.9 copy.28
  156.5 3.4 reshape_reshape.3
  159.9 12.6 %multiply_reduce_fusion = (f32[8,256]{1,0:T(8,128)S(1)}, f32[8,256,2048]{2,1,0:T(8,128)}) fusion(f32[8,256,2048]{2,1,0:T(8,128)} %copy-done, f32[8,256]{1,0:T(8,128)S(1)} %add_bitcast_fusion, pred[256,2048]{1,0:T(8,128)(4,1)S(1)} %bitcast.33, bf16[256,8,32]{0,2,1:T(8,128)(2,1)S(1)} %bitcast.43, bf16[2048,8,32]{0,2,1:T(8,128)(2,1)S(1)} %reshape_reshape.3), kind=kOutput, calls=%fused_computation.1 | convolution fusion | flops 289404928 | bytes 35274752 | tf_op jit(solution)/shard_map/while/body/eval_jaxpr/qhd,khd->hqk/dot_general | solution.py:63
  172.5 14.1 %psum.22 = f32[8,256]{1,0:T(8,128)S(1)} all-reduce(f32[8,256]{1,0:T(8,128)S(1)} %get-tuple-element.60), channel_id=1, replica_groups=mesh['cam'=8,'tile'=32] {'cam'}, use_global_device_ids=true, to_apply=%region_5.6 | all-reduce | flops 2048 | bytes 16384 | tf_op jit(solution)/shard_map/psum | solution.py:72
  186.7 12.2 %multiply_convert_fusion = bf16[8,256,2048]{2,1,0:T(8,128)(2,1)S(1)} fusion(f32[8,256,2048]{2,1,0:T(8,128)} %get-tuple-element.61, f32[8,256,2048]{2,1,0:T(8,128)} %copy-done, f32[8,256]{1,0:T(8,128)S(1)} %psum.22, f32[8,256]{1,0:T(8,128)S(1)} %add_bitcast_fusion, pred[256,2048]{1,0:T(8,128)(4,1)S(1)} %bitcast.34), kind=kLoop, calls=%fused_computation | loop fusion | flops 25165824 | bytes 42483712 | tf_op jit(solution)/shard_map/while/body/eval_jaxpr/convert_element_type | solution.py:77
  198.9 3.2 copy-done.1
  202.1 1.5 convolution_multiply_fusion
  203.6 1.9 copy.30
  205.5 4.8 %pad_maximum_fusion = f32[2048,512]{1,0:T(8,128)} fusion(f32[2048,256]{1,0:T(8,128)} %copy.31, f32[2048,256]{1,0:T(8,128)} %copy.30), kind=kLoop, calls=%fused_computation.8 | loop fusion | flops 1048576 | bytes 8388608 | tf_op jit(solution)/shard_map/concatenate | solution.py:105
  210.3 6.0 %convolution_multiply_fusion.1 = f32[8,256,32]{1,2,0:T(8,128)S(1)} fusion(bf16[8,256,2048]{2,1,0:T(8,128)(2,1)} %copy-done.1, bf16[2048,8,32]{0,2,1:T(8,128)(2,1)S(1)} %bitcast.37), kind=kOutput, calls=%fused_computation.10 | convolution fusion | flops 268500992 | bytes 9699328 | tf_op jit(solution)/shard_map/while/body/eval_jaxpr/hqk,khd->qhd/dot_general | solution.py:81
  216.3 0.1 copy.29
  216.4 33.9 %all-reduce.1 = bf16[256,256]{1,0:T(8,128)(2,1)} all-reduce(f32[256,256]{1,0:T(8,128)S(1)} %copy.29), channel_id=1, replica_groups=mesh['cam'=8,'tile'=32] {'cam'}, use_global_device_ids=true, to_apply=%region_6.7 | all-reduce | flops 65536 | bytes 393216 | tf_op jit(solution)/shard_map/psum | solution.py:107
  250.3 191.3 %reduce-scatter.2.cloned.1.call-done = f32[64,512]{1,0:T(8,128)} async-done(((f32[2048,512]{1,0:T(8,128)}), f32[64,512]{1,0:T(8,128)}) %reduce-scatter.2.cloned.1.call-update) | async-done | bytes 131088 | tf_op jit(solution)/shard_map/reduce_scatter | solution.py:106
  441.6 0.9 convert.4
  442.5 0.6 fusion.10
  (13 shorter events, 0.4 us)
Async XLA Ops:
  7.2 92.1 %all-gather.2.cloned.1.call-start = ((), (), s32[]{:S(2)}) async-start(), calls=%async_computation.2 | async-start | bytes 1081344 | tf_op jit(solution)/shard_map/all_gather | solution.py:15
  9.8 142.9 %all-to-all-start = ((bf16[32,64,256]{2,1,0:T(8,128)(2,1)}), bf16[32,64,256]{2,1,0:T(8,128)(2,1)S(1)}, u32[]{:S(2)}, u32[]{:S(2)}) async-start(bf16[32,64,256]{2,1,0:T(8,128)(2,1)} %stack.2), calls=%async_computation | async-start | bytes 2097152 | tf_op jit(solution)/shard_map/all_to_all | solution.py:17
  22.8 418.7 %reduce-scatter.2.cloned.1.call-start = ((), (), s32[]{:S(2)}) async-start(), calls=%async_computation.3 | async-start | bytes 4325376 | tf_op jit(solution)/shard_map/reduce_scatter | solution.py:106
  104.2 5.7 %copy-start = (f32[8,256,2048]{2,1,0:T(8,128)}, f32[8,256,2048]{2,1,0:T(8,128)S(1)}, u32[]{:S(2)}) copy-start(f32[8,256,2048]{2,1,0:T(8,128)S(1)} %get-tuple-element.59) | copy-start | bytes 50331652
  198.8 3.2 copy-start.1
Sparse Core Ops, SparseCore 0:
  11.4 87.8 all-gather.1
  210.4 231.1 reduce-scatter.1
